TPU v7x, 32 devices: a whole 2x2x4 slice. The times are simulated.
32 devices in a mesh: dp: 8 (over y, x, core), tensor: 4 (over z).
Axes of the slice: x: 2, y: 2, z: 4, core: 2. Of those that a mesh axis runs over, the one named last changes fastest.
Arguments:
- inputs: bfloat16 [2048, 4096], P(('dp', 'tensor')), may hold values from -6 to 6
- out_grad: bfloat16 [2048, 4096], P(('dp', 'tensor')), may hold values from -0.29882812 to 0.29882812
- gate_act: bfloat16 [2048, 14336], P('dp', 'tensor'), may hold values from -6 to 6
- up_act: bfloat16 [2048, 14336], P('dp', 'tensor'), may hold values from -6 to 6
- w_down: bfloat16 [14336, 4096], P('tensor'), may hold values from -0.046875 to 0.046875
- ranks: int32 [3], replicated, may hold values from 8 to 64, as said below
- token_count: int32 [8], P('dp'), may hold values from 128 to 256, as said below
Outputs:
- p_gate: float32 [4, 64, 4096], P('tensor')
- q_gate: float32 [64, 14336], P(None, 'tensor')
- p_up: float32 [4, 64, 4096], P('tensor')
- q_up: float32 [64, 14336], P(None, 'tensor')
- p_down: float32 [64, 14336], P(None, 'tensor')
- q_down: float32 [4, 64, 4096], P('tensor')
Inputs may be any that keep to these rules, and one draw needn't show every extreme that they name: `ranks`: each rank is a multiple of 8; one of the three equals 64 and another 64 / 8. `token_count`: at least one replica has all its tokens live.
All inputs are finite; a program needn't handle non-finite values.
Results may differ from a plain program's by a relative error of at most 0.0063.
Values may be sent and summed in bfloat16 or wider, within the bound.
A program may use at most 128 MiB of HBM per device.

v0:
```python
import jax
import jax.numpy as jnp
from jax import lax
from jax.sharding import PartitionSpec as P

RMAX = 64


def basis(length, rank_value, ranks_total):
    index_rows = jnp.arange(length, dtype=jnp.float32)[:, None]
    index_cols = jnp.arange(ranks_total, dtype=jnp.float32)[None, :]
    table = jnp.cos(jnp.pi * (2.0 * index_rows + 1.0) * index_cols / (2.0 * length)) * jnp.sqrt(
        2.0 / length
    )
    table = jnp.where(index_cols == 0.0, table * jnp.sqrt(0.5), table)
    table = jnp.where(index_cols < rank_value.astype(jnp.float32), table, jnp.zeros_like(table))
    return table.astype(jnp.bfloat16)


def solve_rows(gram, ptrans, rank_value):
    ranks_total = gram.shape[0]
    unused = jnp.where(jnp.arange(ranks_total) < rank_value, 0.0, 1.0).astype(jnp.float32)
    lower = jnp.linalg.cholesky(gram + jnp.diag(unused))
    return lax.linalg.triangular_solve(lower, ptrans, left_side=True, lower=True)


def gram_of(ptrans):
    return jnp.dot(ptrans, ptrans.T, precision=lax.Precision.HIGHEST)


def left_factor(delta, left, basis_table):
    projected = jnp.dot(delta, basis_table, preferred_element_type=jnp.float32).astype(jnp.bfloat16)
    return jnp.dot(projected.T, left, preferred_element_type=jnp.float32)


def right_factor(delta, left, phat):
    back = jnp.dot(left, phat.astype(jnp.bfloat16).T, preferred_element_type=jnp.float32).astype(
        jnp.bfloat16
    )
    return jnp.dot(back.T, delta, preferred_element_type=jnp.float32)


def body(inputs, out_grad, gate_act, up_act, w_down, ranks, token_count):
    inputs_full, grad_full = (
        lax.all_gather(inputs, "tensor", axis=0, tiled=True),
        lax.all_gather(out_grad, "tensor", axis=0, tiled=True),
    )
    total_rows = inputs_full.shape[0]
    live_rows = jnp.arange(total_rows, dtype=jnp.int32) < token_count[0]
    grad_full = jnp.where(live_rows[:, None], grad_full, jnp.zeros_like(grad_full))
    width = w_down.shape[0]
    features = w_down.shape[1]
    ranks_total = RMAX
    hidden_grad = lax.dot_general(
        grad_full, w_down, (((1,), (1,)), ((), ())), preferred_element_type=jnp.float32
    )
    gate = gate_act.astype(jnp.float32)
    upper = up_act.astype(jnp.float32)
    sigmoid_gate = jax.nn.sigmoid(gate)
    silu_gate = gate * sigmoid_gate
    hidden = (silu_gate * upper).astype(jnp.bfloat16)
    d_gate = (hidden_grad * upper * sigmoid_gate * (1.0 + gate * (1.0 - sigmoid_gate))).astype(
        jnp.bfloat16
    )
    d_up = (hidden_grad * silu_gate).astype(jnp.bfloat16)
    basis_gate = basis(width, ranks[0], ranks_total)
    basis_up = basis(width, ranks[1], ranks_total)
    basis_model = basis(features, ranks[2], ranks_total)
    pt_gate = left_factor(d_gate, inputs_full, basis_gate)
    pt_up = left_factor(d_up, inputs_full, basis_up)
    pt_down = left_factor(grad_full, hidden, basis_model)
    sum_gate, sum_up, sum_down = lax.psum((pt_gate, pt_up, pt_down), "dp")
    ph_gate = solve_rows(gram_of(sum_gate), sum_gate, ranks[0])
    ph_up = solve_rows(gram_of(sum_up), sum_up, ranks[1])
    ph_down = solve_rows(gram_of(sum_down), sum_down, ranks[2])
    qt_gate = right_factor(d_gate, inputs_full, ph_gate)
    qt_up = right_factor(d_up, inputs_full, ph_up)
    qt_down = right_factor(grad_full, hidden, ph_down)
    sum_qgate, sum_qup, sum_qdown = lax.psum((qt_gate, qt_up, qt_down), "dp")
    scale_model = jnp.sqrt(jnp.float32(features))
    scale_shard = jnp.sqrt(jnp.float32(width))
    return (
        (ph_gate * scale_model)[None],
        sum_qgate,
        (ph_up * scale_model)[None],
        sum_qup,
        ph_down * scale_shard,
        sum_qdown[None],
    )


def solution(mesh):
    in_specs = (
        P(("dp", "tensor"), None),
        P(("dp", "tensor"), None),
        P("dp", "tensor"),
        P("dp", "tensor"),
        P("tensor", None),
        P(),
        P("dp"),
    )
    out_specs = (
        P("tensor", None, None),
        P(None, "tensor"),
        P("tensor", None, None),
        P(None, "tensor"),
        P(None, "tensor"),
        P("tensor", None, None),
    )
    return jax.shard_map(body, mesh=mesh, in_specs=in_specs, out_specs=out_specs, check_vma=False)
```

profile of v0, /device:TPU:0, one launch (start us, length us, event | category | flops | bytes accessed | tf_op | source)
XLA Modules:
  0.0 343.4 jit_solution(5668337991891124612)
XLA Ops:
  7.2 0.0 all-gather.3.cloned.1.call-start
  7.2 0.7 all-gather.3.cloned.1.call-update
  7.9 0.0 all-gather.5.cloned.1.call-start
  7.9 0.7 all-gather.5.cloned.1.call-update
  8.6 0.0 all-reduce.7.cloned.1.call-start
  9.4 1.4 fusion.104
  12.7 45.5 %all-gather.3.cloned.1.call-done = bf16[256,4096]{1,0:T(8,128)(2,1)} async-done(((bf16[64,4096]{1,0:T(8,128)(2,1)}), bf16[256,4096]{1,0:T(8,128)(2,1)}) %all-gather.3.cloned.1.call-update) | async-done | bytes 2097168 | tf_op jit(solution)/shard_map/all_gather | solution.py:46
  58.2 0.0 copy-start.4
  58.2 12.7 %fusion.10 = f32[64,3584]{1,0:T(8,128)} fusion(f32[4096]{0:T(1024)S(1)} %add_multiply_fusion, pred[64]{0:T(512)(128)(4,1)S(1)} %get-tuple-element.21, pred[64]{0:T(512)(128)(4,1)S(1)} %iota_compare_fusion.3, bf16[256,4096]{1,0:T(8,128)(2,1)} %all-gather.3.cloned.1.call-done, pred[256]{0:T(512)(128)(4,1)S(1)} %iota_compare_fusion.2, ...), kind=kOutput, calls=%fused_computation.26 | convolution fusion | flops 261898240 | bytes 6701440 | tf_op jit(solution)/shard_map/dot_general | solution.py:33
  70.9 0.0 copy-done.4
  70.9 16.8 %multiply_convert_fusion = (bf16[256,3584]{1,0:T(8,128)(2,1)}, bf16[256,3584]{1,0:T(8,128)(2,1)}) fusion(bf16[256,3584]{1,0:T(8,128)(2,1)S(1)} %copy-done.4, bf16[256,3584]{1,0:T(8,128)(2,1)} %param.13, bf16[3584,4096]{1,0:T(8,128)(2,1)} %param.14, bf16[256,4096]{1,0:T(8,128)(2,1)} %all-gather.3.cloned.1.call-done, pred[256]{0:T(512)(128)(4,1)S(1)} %iota_compare_fusion.2), kind=kOutput, calls=%fused_computation.14 | convolution fusion | flops 7531003904 | bytes 38797568 | tf_op jit(solution)/shard_map/dot_general | solution.py:54
  87.7 16.8 %all-gather.5.cloned.1.call-done = bf16[256,4096]{1,0:T(8,128)(2,1)} async-done(((bf16[64,4096]{1,0:T(8,128)(2,1)}), bf16[256,4096]{1,0:T(8,128)(2,1)}) %all-gather.5.cloned.1.call-update) | async-done | bytes 2097168 | tf_op jit(solution)/shard_map/all_gather | solution.py:45
  104.5 0.0 copy-start.2
  104.5 10.4 %fusion.9 = f32[64,4096]{1,0:T(8,128)} fusion(bf16[256,4096]{1,0:T(8,128)(2,1)} %all-gather.5.cloned.1.call-done, bf16[256,3584]{1,0:T(8,128)(2,1)} %get-tuple-element.14, f32[3584]{0:T(1024)S(1)} %add_multiply_fusion.1, pred[64]{0:T(512)(128)(4,1)S(1)} %iota_compare_fusion.4, pred[64]{0:T(512)(128)(4,1)S(1)} %get-tuple-element.21), kind=kOutput, calls=%fused_computation.25 | convolution fusion | flops 253280256 | bytes 4995200 | tf_op jit(solution)/shard_map/dot_general | solution.py:33
  114.9 0.0 copy-done.2
  114.9 19.9 %fusion.8 = f32[64,4096]{1,0:T(8,128)} fusion(bf16[256,4096]{1,0:T(8,128)(2,1)S(1)} %copy-done.2, bf16[256,3584]{1,0:T(8,128)(2,1)} %get-tuple-element.15, f32[3584]{0:T(1024)S(1)} %add_multiply_fusion.1, pred[64]{0:T(512)(128)(4,1)S(1)} %get-tuple-element.21, pred[64]{0:T(512)(128)(4,1)S(1)} %get-tuple-element.22), kind=kOutput, calls=%fused_computation.24 | convolution fusion | flops 253280256 | bytes 4995200 | tf_op jit(solution)/shard_map/dot_general | solution.py:33
  134.8 0.0 all-reduce.7.cloned.1.call-update
  134.9 0.0 all-reduce.5.cloned.1.call-start
  134.9 0.7 compare_select_fusion
  135.6 0.7 compare_select_fusion.2
  136.2 0.7 compare_select_fusion.1
  136.9 65.4 %all-reduce.7.cloned.1.call-done = (f32[64,4096]{1,0:T(8,128)}, f32[64,4096]{1,0:T(8,128)}, f32[64,3584]{1,0:T(8,128)}) async-done(((f32[64,4096]{1,0:T(8,128)}, f32[64,4096]{1,0:T(8,128)}, f32[64,3584]{1,0:T(8,128)}), (f32[64,4096]{1,0:T(8,128)}, f32[64,4096]{1,0:T(8,128)}, f32[64,3584]{1,0:T(8,128)})) %all-reduce.7.cloned.1.call-update) | async-done | bytes 3014672 | tf_op jit(solution)/shard_map/psum | solution.py:72
  202.3 0.0 copy-start.1
  202.3 2.4 convolution_add_fusion
  204.8 0.1 copy.17
  204.9 0.1 copy.18
  204.9 5.9 %cholesky.81 = f32[64,64]{1,0:T(8,128)S(1)} custom-call(f32[64,64]{1,0:T(8,128)S(1)} %copy.18), custom_call_target="Cholesky" | custom-call | tf_op jit(solution)/shard_map/jit(cholesky)/cholesky | solution.py:23
  210.8 0.6 compare_reduce_fusion
  211.5 0.7 fusion.63
  212.1 4.9 %custom-call.8 = f32[1,64,64]{1,2,0:T(8,128)S(1)} custom-call(f32[1,64,64]{2,1,0:T(8,128)S(1)} %fusion.63), custom_call_target="InvertDiagBlocksLowerTriangular" | custom-call | tf_op jit(solution)/shard_map/triangular_solve | solution.py:24
  217.0 0.0 copy-done.1
  217.1 0.0 copy-start
  217.1 1.0 convolution_add_fusion.1
  218.1 0.1 copy.15
  218.1 0.1 copy.16
  218.2 5.9 %cholesky.70 = f32[64,64]{1,0:T(8,128)S(1)} custom-call(f32[64,64]{1,0:T(8,128)S(1)} %copy.16), custom_call_target="Cholesky" | custom-call | tf_op jit(solution)/shard_map/jit(cholesky)/cholesky | solution.py:23
  224.1 0.6 compare_reduce_fusion.1
  224.8 0.7 fusion.62
  225.4 4.9 %custom-call.11 = f32[1,64,64]{1,2,0:T(8,128)S(1)} custom-call(f32[1,64,64]{2,1,0:T(8,128)S(1)} %fusion.62), custom_call_target="InvertDiagBlocksLowerTriangular" | custom-call | tf_op jit(solution)/shard_map/triangular_solve/custom-call.0 | solution.py:24
  230.3 1.0 fusion.67
  231.4 0.0 copy-done
  231.4 1.0 convolution_add_fusion.2
  232.4 0.1 copy.13
  232.5 0.1 copy.14
  232.5 5.9 %cholesky.59 = f32[64,64]{1,0:T(8,128)S(1)} custom-call(f32[64,64]{1,0:T(8,128)S(1)} %copy.14), custom_call_target="Cholesky" | custom-call | tf_op jit(solution)/shard_map/jit(cholesky)/cholesky | solution.py:23
  238.4 0.6 compare_reduce_fusion.2
  239.1 0.7 fusion.61
  239.7 4.9 %custom-call.10 = f32[1,64,64]{1,2,0:T(8,128)S(1)} custom-call(f32[1,64,64]{2,1,0:T(8,128)S(1)} %fusion.61), custom_call_target="InvertDiagBlocksLowerTriangular" | custom-call | tf_op jit(solution)/shard_map/triangular_solve/custom-call.0 | solution.py:24
  244.6 1.0 fusion.70
  245.7 3.0 broadcast_multiply_fusion
  248.7 4.8 %fusion.12 = f32[64,3584]{1,0:T(8,128)} fusion(bf16[256,3584]{1,0:T(8,128)(2,1)} %get-tuple-element.14, bf16[256,4096]{1,0:T(8,128)(2,1)} %all-gather.5.cloned.1.call-done, f32[64,4096]{1,0:T(8,128)S(1)} %fusion.67), kind=kOutput, calls=%fused_computation.30 | convolution fusion | flops 251936768 | bytes 5898240 | tf_op jit(solution)/shard_map/dot_general | solution.py:40
  253.5 4.6 %fusion.11 = f32[64,3584]{1,0:T(8,128)} fusion(bf16[256,3584]{1,0:T(8,128)(2,1)} %get-tuple-element.15, bf16[256,4096]{1,0:T(8,128)(2,1)} %all-gather.5.cloned.1.call-done, f32[64,4096]{1,0:T(8,128)S(1)} %fusion.70), kind=kOutput, calls=%fused_computation.29 | convolution fusion | flops 251936768 | bytes 5898240 | tf_op jit(solution)/shard_map/dot_general | solution.py:40
  258.1 5.6 %convolution_bitcast_fusion = f32[1,64,4096]{2,1,0:T(8,128)} fusion(bf16[64,3584]{1,0:T(8,128)(2,1)S(1)} %get-tuple-element.20, bf16[256,4096]{1,0:T(8,128)(2,1)} %all-gather.3.cloned.1.call-done, pred[256]{0:T(512)(128)(4,1)S(1)} %iota_compare_fusion.2, bf16[256,3584]{1,0:T(8,128)(2,1)} %param.13, bf16[256,3584]{1,0:T(8,128)(2,1)} %param.12), kind=kOutput, calls=%fused_computation.3 | convolution fusion | flops 260063232 | bytes 7274752 | tf_op jit(solution)/shard_map/dot_general | solution.py:40
  263.7 0.0 all-reduce.5.cloned.1.call-update
  263.7 1.1 multiply_bitcast_fusion
  264.8 1.1 multiply_bitcast_fusion.1
  265.9 65.4 %all-reduce.5.cloned.1.call-done = (f32[64,3584]{1,0:T(8,128)}, f32[64,3584]{1,0:T(8,128)}, f32[1,64,4096]{2,1,0:T(8,128)}) async-done(((f32[64,3584]{1,0:T(8,128)}, f32[64,3584]{1,0:T(8,128)}, f32[1,64,4096]{2,1,0:T(8,128)}), (f32[64,3584]{1,0:T(8,128)}, f32[64,3584]{1,0:T(8,128)}, f32[1,64,4096]{2,1,0:T(8,128)})) %all-reduce.5.cloned.1.call-update) | async-done | bytes 2883600 | tf_op jit(solution)/shard_map/psum | solution.py:79
  331.2 0.0 copy-start.3
  331.2 2.3 copy.26
  333.5 2.2 copy.27
  335.6 0.0 copy-done.3
  335.6 1.0 copy.28
  (12 shorter events, 0.2 us)
Async XLA Ops:
  7.2 51.1 %all-gather.3.cloned.1.call-start = ((), (), s32[]{:S(2)}) async-start(), calls=%async_computation | async-start | bytes 2621440 | tf_op jit(solution)/shard_map/all_gather | solution.py:46
  7.9 96.6 %all-gather.5.cloned.1.call-start = ((), (), s32[]{:S(2)}) async-start(), calls=%async_computation.1 | async-start | bytes 2621440 | tf_op jit(solution)/shard_map/all_gather | solution.py:45
  8.6 193.7 %all-reduce.7.cloned.1.call-start = ((), (), s32[]{:S(2)}) async-start(), calls=%async_computation.3 | async-start | bytes 6029312 | tf_op jit(solution)/shard_map/psum | solution.py:72
  58.2 12.7 %copy-start.4 = (bf16[256,3584]{1,0:T(8,128)(2,1)S(1)}, bf16[256,3584]{1,0:T(8,128)(2,1)}, u32[]{:S(2)}) copy-start(bf16[256,3584]{1,0:T(8,128)(2,1)} %param.12) | copy-start | bytes 5505028
  104.5 10.4 %copy-start.2 = (bf16[256,4096]{1,0:T(8,128)(2,1)S(1)}, bf16[256,4096]{1,0:T(8,128)(2,1)}, u32[]{:S(2)}) copy-start(bf16[256,4096]{1,0:T(8,128)(2,1)} %all-gather.5.cloned.1.call-done) | copy-start | bytes 6291460
  134.9 196.4 %all-reduce.5.cloned.1.call-start = ((), (), s32[]{:S(2)}) async-start(), calls=%async_computation.2 | async-start | bytes 5767168 | tf_op jit(solution)/shard_map/psum | solution.py:79
  202.3 14.7 %copy-start.1 = (f32[64,4096]{1,0:T(8,128)S(1)}, f32[64,4096]{1,0:T(8,128)}, u32[]{:S(2)}) copy-start(f32[64,4096]{1,0:T(8,128)} %get-tuple-element.12) | copy-start | bytes 3145732
  217.1 14.3 %copy-start = (f32[64,4096]{1,0:T(8,128)S(1)}, f32[64,4096]{1,0:T(8,128)}, u32[]{:S(2)}) copy-start(f32[64,4096]{1,0:T(8,128)} %get-tuple-element.11) | copy-start | bytes 3145732
  331.2 4.4 %copy-start.3 = (f32[1,64,4096]{2,1,0:T(8,128)S(1)}, f32[1,64,4096]{2,1,0:T(8,128)}, u32[]{:S(2)}) copy-start(f32[1,64,4096]{2,1,0:T(8,128)} %get-tuple-element.30) | copy-start | bytes 3145732
Sparse Core Ops, SparseCore 0:
  9.6 48.6 all-gather.2
  59.8 44.6 all-gather.4
  135.0 67.2 all-reduce.6
  263.9 67.3 all-reduce.4
where the time goes:
time: 346 us; the launch traced here: 343 us
  waiting for transfers between devices  194 us (56%)
  matrix products  84.3 us (24%)
  other arithmetic  40.4 us (12%)
  between operations  16.8 us (5%)
  local copies, waits for them, and re-layouts  7.22 us (2%)
    psum x1, waiting for transfers between devices, body(): sum_gate, sum_up, sum_down = lax.psum((pt_gate, pt_up, pt_down), 'dp')  65.4 us
    psum x1, waiting for transfers between devices, body(): sum_qgate, sum_qup, sum_qdown = lax.psum((qt_gate, qt_up, qt_down), 'dp')  65.4 us
    all_gather x1, waiting for transfers between devices, body(): lax.all_gather(out_grad, 'tensor', axis=0, tiled=True)  45.5 us
    dot_general x3, matrix products, left_factor(): return jnp.dot(projected.T, left, preferred_element_type=jnp.float32)  43 us
    another operation x9, other arithmetic, solve_rows(): lower = jnp.linalg.cholesky(gram + jnp.diag(unused))  19.6 us
    dot_general x1, matrix products, body(): lax.dot_general(grad_full, w_down, (((1,), (1,)), ((), ())), preferred_el...  16.8 us
    all_gather x1, waiting for transfers between devices, body(): lax.all_gather(inputs, 'tensor', axis=0, tiled=True)  16.8 us
    another operation x6, other arithmetic, solve_rows(): lax.linalg.triangular_solve(lower, ptrans, left_side=True, lower=True)  16.6 us
  transfers between devices with their start and end apart: 4, of which 4 were waited for; matrix products, arithmetic and copies ran while one was open for 10% of the time, Pallas kernels for 0%

commit v1 on v0

--- a/solution.py
+++ b/solution.py
@@ -1,9 +1,21 @@
+import functools
+
 import jax
 import jax.numpy as jnp
+import ml_dtypes
+import numpy as np
 from jax import lax
+from jax.experimental import pallas as pl
+from jax.experimental.pallas import tpu as pltpu
 from jax.sharding import PartitionSpec as P
 
 RMAX = 64
+BF = jnp.bfloat16
+F32 = jnp.float32
+MESH = pl.DeviceIdType.MESH
+TILE = 512
+CHUNK = 16
+MIB = 1024 * 1024
 
 
 def basis(length, rank_value, ranks_total):
@@ -40,7 +52,7 @@
     return jnp.dot(back.T, delta, preferred_element_type=jnp.float32)
 
 
-def body(inputs, out_grad, gate_act, up_act, w_down, ranks, token_count):
+def general_body(inputs, out_grad, gate_act, up_act, w_down, ranks, token_count):
     inputs_full, grad_full = (
         lax.all_gather(inputs, "tensor", axis=0, tiled=True),
         lax.all_gather(out_grad, "tensor", axis=0, tiled=True),
@@ -63,12 +75,9 @@
         jnp.bfloat16
     )
     d_up = (hidden_grad * silu_gate).astype(jnp.bfloat16)
-    basis_gate = basis(width, ranks[0], ranks_total)
-    basis_up = basis(width, ranks[1], ranks_total)
-    basis_model = basis(features, ranks[2], ranks_total)
-    pt_gate = left_factor(d_gate, inputs_full, basis_gate)
-    pt_up = left_factor(d_up, inputs_full, basis_up)
-    pt_down = left_factor(grad_full, hidden, basis_model)
+    pt_gate = left_factor(d_gate, inputs_full, basis(width, ranks[0], ranks_total))
+    pt_up = left_factor(d_up, inputs_full, basis(width, ranks[1], ranks_total))
+    pt_down = left_factor(grad_full, hidden, basis(features, ranks[2], ranks_total))
     sum_gate, sum_up, sum_down = lax.psum((pt_gate, pt_up, pt_down), "dp")
     ph_gate = solve_rows(gram_of(sum_gate), sum_gate, ranks[0])
     ph_up = solve_rows(gram_of(sum_up), sum_up, ranks[1])
@@ -89,6 +98,469 @@
     )
 
 
+def table_of(length):
+    rows = np.arange(length, dtype=np.float64)[:, None]
+    cols = np.arange(RMAX, dtype=np.float64)[None, :]
+    table = np.cos(np.pi * (2.0 * rows + 1.0) * cols / (2.0 * length)) * np.sqrt(2.0 / length)
+    table[:, 0] *= np.sqrt(0.5)
+    return table.astype(np.float32).astype(ml_dtypes.bfloat16)
+
+
+def dot(left, right, dims):
+    return lax.dot_general(left, right, ((dims[:1], dims[1:]), ((), ())), preferred_element_type=F32)
+
+
+def columns(index, width):
+    return pl.ds(pl.multiple_of(index * width, 128), width)
+
+
+def front_kernel(
+    n, x_hbm, g_hbm, gate_hbm, up_hbm, w_hbm, bw_ref, bm_ref, mask_ref,
+    x_full, g_full, hid, d_gate, d_up, pt_a, pt_b,
+    w_vmem, gate_v, up_v, acc, proj_a, proj_b,
+    load_sem, w_sem, own_sem, send_sem, recv_sem,
+):
+    me = lax.axis_index("tensor")
+    rows = x_hbm.shape[0]
+    pieces = rows // CHUNK
+    width, features = w_hbm.shape
+    tiles = width // TILE
+
+    w_loads = [
+        pltpu.make_async_copy(
+            w_hbm.at[pl.ds(i * TILE, TILE)], w_vmem.at[pl.ds(i * TILE, TILE)], w_sem.at[i]
+        )
+        for i in range(tiles)
+    ]
+    own = []
+    for a, (hbm, full) in enumerate(((g_hbm, g_full), (x_hbm, x_full))):
+        mine = pl.ds(pl.multiple_of(me * rows, rows), rows)
+        own.append(pltpu.make_async_copy(hbm, full.at[mine], own_sem.at[a]))
+    loads = [
+        pltpu.make_async_copy(gate_hbm, gate_v, load_sem.at[0]),
+        pltpu.make_async_copy(up_hbm, up_v, load_sem.at[1]),
+    ]
+
+    barrier = pltpu.get_barrier_semaphore()
+
+    @pl.when(me > 0)
+    def _():
+        pl.semaphore_signal(barrier, inc=1, device_id={"tensor": me - 1}, device_id_type=MESH)
+
+    @pl.when(me < n - 1)
+    def _():
+        pl.semaphore_signal(barrier, inc=1, device_id={"tensor": me + 1}, device_id_type=MESH)
+
+    inside = jnp.logical_and(me > 0, me < n - 1)
+
+    @pl.when(inside)
+    def _():
+        pl.semaphore_wait(barrier, 2)
+
+    @pl.when(jnp.logical_not(inside))
+    def _():
+        pl.semaphore_wait(barrier, 1)
+
+    fulls = (g_full, x_full)
+    hbms = (g_hbm, x_hbm)
+
+    def copy(a, side, shard, piece, first):
+        place = fulls[a].at[pl.ds(pl.multiple_of(shard * rows + piece * CHUNK, CHUNK), CHUNK)]
+        source = place
+        if first:
+            source = hbms[a].at[pl.ds(pl.multiple_of(piece * CHUNK, CHUNK), CHUNK)]
+        return pltpu.make_async_remote_copy(
+            src_ref=source,
+            dst_ref=place,
+            send_sem=send_sem.at[a, side, shard, piece],
+            recv_sem=recv_sem.at[a, shard, piece],
+            device_id={"tensor": me + 1 if side == 0 else me - 1},
+            device_id_type=MESH,
+        )
+
+    def step(a, d, piece):
+        right, left = me - d, me + d
+        if d == 0:
+            @pl.when(me < n - 1)
+            def _():
+                copy(a, 0, me, piece, True).start()
+
+            @pl.when(me > 0)
+            def _():
+                copy(a, 1, me, piece, True).start()
+
+            return
+
+        @pl.when(right >= 0)
+        def _():
+            copy(a, 1, right, piece, False).wait_recv()
+
+            @pl.when(me < n - 1)
+            def _():
+                copy(a, 0, right, piece, False).start()
+
+        @pl.when(left < n)
+        def _():
+            copy(a, 0, left, piece, False).wait_recv()
+
+            @pl.when(me > 0)
+            def _():
+                copy(a, 1, left, piece, False).start()
+
+    def each_piece(a, d):
+        def run(piece, carry):
+            step(a, d, piece)
+            return carry
+
+        lax.fori_loop(0, pieces, run, 0)
+
+    each_piece(0, 0)
+    for item in own + loads + w_loads:
+        item.start()
+    for d in range(1, n - 1):
+        each_piece(0, d)
+    each_piece(1, 0)
+    each_piece(0, n - 1)
+    for item in own + loads + w_loads:
+        item.wait()
+
+    proj_b[...] = (dot(g_full[...], bm_ref[...], (1, 0)) * mask_ref[2:3, :]).astype(BF)
+    acc[...] = jnp.zeros_like(acc)
+
+    def tile(i, carry):
+        cols = columns(i, TILE)
+        taken = pl.ds(pl.multiple_of(i * TILE, TILE), TILE)
+        hg = dot(g_full[...], w_vmem[taken, :], (1, 1))
+        gate = gate_v[:, cols].astype(F32)
+        upper = up_v[:, cols].astype(F32)
+        sig = 1.0 / (1.0 + jnp.exp(-gate))
+        silu = gate * sig
+        hidden = (silu * upper).astype(BF)
+        dg = (hg * upper * sig * (1.0 + gate * (1.0 - sig))).astype(BF)
+        du = (hg * silu).astype(BF)
+        hid[:, cols] = hidden
+        d_gate[:, cols] = dg
+        d_up[:, cols] = du
+        table = bw_ref[taken, :]
+        acc[0] += dot(dg, table, (1, 0))
+        acc[1] += dot(du, table, (1, 0))
+        pt_b[:, cols] = dot(proj_b[...], hidden, (0, 0)).astype(BF)
+
+        @pl.when(jnp.logical_and(i >= 2, i < 2 + pieces))
+        def _():
+            step(1, 1, i - 2)
+
+        return carry
+
+    lax.fori_loop(0, tiles, tile, 0)
+    for d in range(2, n):
+        each_piece(1, d)
+
+    for k in range(2):
+        proj_a[k] = (acc[k] * mask_ref[k:k + 1, :]).astype(BF)
+
+    def left(i, carry):
+        cols = columns(i, TILE)
+        block = x_full[:, cols]
+        for k in range(2):
+            pt_a[k * RMAX:(k + 1) * RMAX, cols] = dot(proj_a[k], block, (0, 0)).astype(BF)
+        return carry
+
+    lax.fori_loop(0, features // TILE, left, 0)
+
+    for a in range(2):
+        for d in range(n):
+            def drain(piece, carry, a=a, d=d):
+                @pl.when(jnp.logical_and(me - d >= 0, me < n - 1))
+                def _():
+                    copy(a, 0, me - d, piece, d == 0).wait_send()
+
+                @pl.when(jnp.logical_and(me + d < n, me > 0))
+                def _():
+                    copy(a, 1, me + d, piece, d == 0).wait_send()
+
+                return carry
+
+            lax.fori_loop(0, pieces, drain, 0)
+
+
+def sum_kernel(
+    a_ref, b_ref, oa_ref, ob_ref, sib_a, sib_b, mid_a, mid_b, got_a, got_b,
+    pair_send, pair_recv, rs_send, rs_recv, ag_send, ag_recv, out_send, out_recv,
+):
+    me = lax.axis_index("dp")
+    core = lax.rem(me, 2)
+    chip = me // 2
+    sibling = chip * 2 + 1 - core
+    others = (3 - chip, chip + 1 - 2 * lax.rem(chip, 2), lax.rem(chip + 2, 4))
+
+    barrier = pltpu.get_barrier_semaphore()
+    pl.semaphore_signal(barrier, inc=1, device_id={"dp": sibling}, device_id_type=MESH)
+    for other in others:
+        pl.semaphore_signal(barrier, inc=1, device_id={"dp": other * 2 + core}, device_id_type=MESH)
+    pl.semaphore_wait(barrier, 4)
+
+    def remote(src, dst, send, recv, device):
+        return pltpu.make_async_remote_copy(
+            src_ref=src, dst_ref=dst, send_sem=send, recv_sem=recv,
+            device_id={"dp": device}, device_id_type=MESH,
+        )
+
+    arrays = (
+        (a_ref, oa_ref, sib_a, mid_a, got_a),
+        (b_ref, ob_ref, sib_b, mid_b, got_b),
+    )
+    started = []
+    pairs = []
+    for n, (src, out, sib, mid, got) in enumerate(arrays):
+        half = src.shape[1] // 2
+        item = remote(src.at[:, columns(1 - core, half)], sib, pair_send.at[n], pair_recv.at[n], sibling)
+        item.start()
+        pairs.append(item)
+        started.append(item)
+    scattered = []
+    for n, (src, out, sib, mid, got) in enumerate(arrays):
+        half = src.shape[1] // 2
+        part = src.shape[0] // 4
+        pairs[n].wait_recv()
+        mid[...] = (src[:, columns(core, half)].astype(F32) + sib[...].astype(F32)).astype(BF)
+        for k, other in enumerate(others):
+            rows = pl.ds(pl.multiple_of(other * part, part), part)
+            item = remote(mid.at[rows], got.at[k], rs_send.at[n, k], rs_recv.at[n, k], other * 2 + core)
+            item.start()
+            scattered.append(item)
+            started.append(item)
+    gathered = []
+    handed = []
+    for n, (src, out, sib, mid, got) in enumerate(arrays):
+        half = src.shape[1] // 2
+        part = src.shape[0] // 4
+        rows = pl.ds(pl.multiple_of(chip * part, part), part)
+        cols = columns(core, half)
+        total = src[rows, cols].astype(F32) + sib[rows, :].astype(F32)
+        for k in range(3):
+            scattered[3 * n + k].wait_recv()
+            total = total + got[k].astype(F32)
+        out[rows, cols] = total.astype(BF)
+        block = out.at[rows, cols]
+        for k, other in enumerate(others):
+            item = remote(block, block, ag_send.at[n, k], ag_recv.at[n, k], other * 2 + core)
+            item.start()
+            gathered.append(item)
+            started.append(item)
+        item = remote(block, block, out_send.at[n, 3], out_recv.at[n, 3], sibling)
+        item.start()
+        handed.append(item)
+        started.append(item)
+    for n, (src, out, sib, mid, got) in enumerate(arrays):
+        half = src.shape[1] // 2
+        part = src.shape[0] // 4
+        for k in (1, 2, 0):
+            gathered[3 * n + k].wait_recv()
+            block = out.at[pl.ds(pl.multiple_of(others[k] * part, part), part), columns(core, half)]
+            item = remote(block, block, out_send.at[n, k], out_recv.at[n, k], sibling)
+            item.start()
+            handed.append(item)
+            started.append(item)
+    for item in handed:
+        item.wait_recv()
+    for item in started:
+        item.wait_send()
+
+
+def dp_sum(a, b, number):
+    def half(array):
+        return pltpu.VMEM((array.shape[0], array.shape[1] // 2), BF)
+
+    def got(array):
+        return pltpu.VMEM((3, array.shape[0] // 4, array.shape[1] // 2), BF)
+
+    dma = pltpu.SemaphoreType.DMA
+    return pl.pallas_call(
+        sum_kernel,
+        out_shape=[jax.ShapeDtypeStruct(a.shape, BF), jax.ShapeDtypeStruct(b.shape, BF)],
+        in_specs=[pl.BlockSpec(memory_space=pltpu.VMEM)] * 2,
+        out_specs=[pl.BlockSpec(memory_space=pltpu.VMEM)] * 2,
+        scratch_shapes=[
+            half(a), half(b), half(a), half(b), got(a), got(b),
+            dma((2,)), dma((2,)), dma((2, 3)), dma((2, 3)), dma((2, 3)), dma((2, 3)),
+            dma((2, 4)), dma((2, 4)),
+        ],
+        compiler_params=pltpu.CompilerParams(
+            collective_id=number, has_side_effects=True, vmem_limit_bytes=32 * MIB
+        ),
+        name="dp_sum_%d" % number,
+    )(a, b)
+
+
+def inverse_factors(grams):
+    size = RMAX
+    row = lax.broadcasted_iota(jnp.int32, (size, size), 0)
+    col = lax.broadcasted_iota(jnp.int32, (size, size), 1)
+    eye = jnp.where(row == col, 1.0, 0.0).astype(F32)
+    sub = lax.broadcasted_iota(jnp.int32, (8, 2 * size), 0)
+    state = []
+    for gram in grams:
+        joined = jnp.concatenate([eye, gram], axis=1)
+        state.append([joined[8 * b:8 * b + 8] for b in range(size // 8)])
+    for k in range(size):
+        kb, kr = k // 8, k % 8
+        for blocks in state:
+            pivot_row = blocks[kb][kr:kr + 1, :]
+            inv = lax.rsqrt(pivot_row[:, size + k:size + k + 1])
+            scaled = pivot_row * inv
+            twice = scaled * inv
+            for b in range(kb, size // 8):
+                block = blocks[b]
+                new = block - block[:, size + k:size + k + 1] * twice
+                if b == kb:
+                    new = jnp.where(sub > kr, new, jnp.where(sub == kr, scaled, block))
+                blocks[b] = new
+    return [jnp.concatenate(blocks, axis=0)[:, :size] for blocks in state]
+
+
+def back_kernel(
+    pa_ref, pb_ref, unused_ref, x_hbm, g_hbm, hid_hbm, dg_hbm, du_hbm,
+    p_gate, p_up, p_down, qa, qb,
+    x_v, g_v, hid_v, dg_v, du_v, pha, phb, split, sem,
+):
+    loads = [
+        pltpu.make_async_copy(src, dst, sem.at[i])
+        for i, (src, dst) in enumerate(
+            ((x_hbm, x_v), (hid_hbm, hid_v), (g_hbm, g_v), (dg_hbm, dg_v), (du_hbm, du_v))
+        )
+    ]
+    for item in loads:
+        item.start()
+    features = pa_ref.shape[1]
+    width = pb_ref.shape[1]
+    size = RMAX
+    row = lax.broadcasted_iota(jnp.int32, (size, size), 0)
+    col = lax.broadcasted_iota(jnp.int32, (size, size), 1)
+    both = dot(pa_ref[...], pa_ref[...], (1, 1))
+    grams = [both[:size, :size], both[size:, size:], dot(pb_ref[...], pb_ref[...], (1, 1))]
+    for k in range(3):
+        grams[k] = grams[k] + jnp.where(row == col, unused_ref[k:k + 1, :], 0.0)
+    for k, inverse in enumerate(inverse_factors(grams)):
+        high = inverse.astype(BF)
+        split[k, 0] = high
+        split[k, 1] = (inverse - high.astype(F32)).astype(BF)
+
+    def solve(k, block):
+        return dot(split[k, 0], block, (1, 0)) + dot(split[k, 1], block, (1, 0))
+
+    def wide(i, carry):
+        cols = columns(i, TILE)
+        for k, out in enumerate((p_gate, p_up)):
+            ph = solve(k, pa_ref[k * size:(k + 1) * size, cols])
+            out[0, :, cols] = ph * np.float32(np.sqrt(features))
+            pha[k * size:(k + 1) * size, cols] = ph.astype(BF)
+        return carry
+
+    lax.fori_loop(0, features // TILE, wide, 0)
+
+    def narrow(i, carry):
+        cols = columns(i, TILE)
+        ph = solve(2, pb_ref[:, cols])
+        p_down[:, cols] = ph * np.float32(np.sqrt(width))
+        phb[:, cols] = ph.astype(BF)
+        return carry
+
+    lax.fori_loop(0, width // TILE, narrow, 0)
+    for item in loads:
+        item.wait()
+    back_a = dot(x_v[...], pha[...], (1, 1)).astype(BF)
+    back_b = dot(hid_v[...], phb[...], (1, 1)).astype(BF)
+
+    def right(i, carry):
+        cols = columns(i, TILE)
+        qa[:size, cols] = dot(back_a[:, :size], dg_v[:, cols], (0, 0)).astype(BF)
+        qa[size:, cols] = dot(back_a[:, size:], du_v[:, cols], (0, 0)).astype(BF)
+        return carry
+
+    lax.fori_loop(0, width // TILE, right, 0)
+
+    def right_down(i, carry):
+        cols = columns(i, TILE)
+        qb[:, cols] = dot(back_b, g_v[:, cols], (0, 0)).astype(BF)
+        return carry
+
+    lax.fori_loop(0, features // TILE, right_down, 0)
+
+
+def kernel_body(n, inputs, out_grad, gate_act, up_act, w_down, ranks, token_count):
+    rows, features = inputs.shape
+    width = w_down.shape[0]
+    total = rows * n
+    tiles = width // TILE
+    pieces = rows // CHUNK
+    here = lax.axis_index("tensor") * rows + jnp.arange(rows, dtype=jnp.int32)
+    masked = jnp.where((here < token_count[0])[:, None], out_grad, jnp.zeros_like(out_grad))
+    used = jnp.arange(RMAX)[None, :] < ranks[:, None]
+    mask = used.astype(F32)
+    unused = 1.0 - mask
+    dma = pltpu.SemaphoreType.DMA
+    vmem = pl.BlockSpec(memory_space=pltpu.VMEM)
+    hbm = pl.BlockSpec(memory_space=pl.ANY)
+
+    def shape(*dims):
+        return jax.ShapeDtypeStruct(dims, BF)
+
+    x_full, g_full, hid, d_gate, d_up, pt_a, pt_b = pl.pallas_call(
+        functools.partial(front_kernel, n),
+        out_shape=[
+            shape(total, features), shape(total, features), shape(total, width),
+            shape(total, width), shape(total, width), shape(2 * RMAX, features), shape(RMAX, width),
+        ],
+        in_specs=[hbm] * 5 + [vmem] * 3,
+        out_specs=[vmem] * 7,
+        scratch_shapes=[
+            pltpu.VMEM((width, features), BF),
+            pltpu.VMEM((total, width), BF),
+            pltpu.VMEM((total, width), BF),
+            pltpu.VMEM((2, total, RMAX), F32),
+            pltpu.VMEM((2, total, RMAX), BF),
+            pltpu.VMEM((total, RMAX), BF),
+            dma((2,)), dma((tiles,)), dma((2,)),
+            dma((2, 2, n, pieces)), dma((2, n, pieces)),
+        ],
+        compiler_params=pltpu.CompilerParams(
+            collective_id=0, has_side_effects=True, vmem_limit_bytes=60 * MIB
+        ),
+        name="front",
+    )(inputs, masked, gate_act, up_act, w_down, jnp.asarray(table_of(width)),
+      jnp.asarray(table_of(features)), mask)
+
+    sum_a, sum_b = dp_sum(pt_a, pt_b, 1)
+
+    p_gate, p_up, p_down, qa, qb = pl.pallas_call(
+        back_kernel,
+        out_shape=[
+            jax.ShapeDtypeStruct((1, RMAX, features), F32),
+            jax.ShapeDtypeStruct((1, RMAX, features), F32),
+            jax.ShapeDtypeStruct((RMAX, width), F32),
+            shape(2 * RMAX, width), shape(RMAX, features),
+        ],
+        in_specs=[vmem] * 3 + [hbm] * 5,
+        out_specs=[vmem] * 5,
+        scratch_shapes=[
+            pltpu.VMEM((total, features), BF), pltpu.VMEM((total, features), BF),
+            pltpu.VMEM((total, width), BF), pltpu.VMEM((total, width), BF),
+            pltpu.VMEM((total, width), BF),
+            pltpu.VMEM((2 * RMAX, features), BF), pltpu.VMEM((RMAX, width), BF),
+            pltpu.VMEM((3, 2, RMAX, RMAX), BF),
+            dma((5,)),
+        ],
+        compiler_params=pltpu.CompilerParams(vmem_limit_bytes=48 * MIB),
+        name="back",
+    )(sum_a, sum_b, unused, x_full, g_full, hid, d_gate, d_up)
+
+    qa, qb = dp_sum(qa, qb, 2)
+    return (
+        p_gate, qa[:RMAX].astype(F32), p_up, qa[RMAX:].astype(F32), p_down, qb.astype(F32)[None],
+    )
+
+
 def solution(mesh):
     in_specs = (
         P(("dp", "tensor"), None),
@@ -107,4 +579,7 @@
         P(None, "tensor"),
         P("tensor", None, None),
     )
+    body = general_body
+    if mesh.shape["dp"] == 8 and mesh.shape["tensor"] == 4:
+        body = functools.partial(kernel_body, mesh.shape["tensor"])
     return jax.shard_map(body, mesh=mesh, in_specs=in_specs, out_specs=out_specs, check_vma=False)

time: 346 us -> 154 us (0.45)
  waiting for transfers between devices: 194 us -> 0 us
  Pallas kernels: 0 us -> 142 us
  matrix products: 84.3 us -> 0 us
  other arithmetic: 40.4 us -> 6.42 us
  between operations: 16.8 us -> 1.34 us
  local copies, waits for them, and re-layouts: 7.22 us -> 3.73 us
    pallas_call x0 -> x4, Pallas kernels: none -> 142 us  [the longest x1 81.6 us: kernel_body(): pl.pallas_call(functools.partial(front_kernel, n), out_shape=[shape(total...]
    psum x2 -> x0, waiting for transfers between devices: 131 us -> none  [the longest x1 65.4 us: body(): sum_gate, sum_up, sum_down = lax.psum((pt_gate, pt_up, pt_down), 'dp')]
    dot_general x10 -> x0, matrix products: 79.2 us -> none  [the longest x3 43 us: left_factor(): return jnp.dot(projected.T, left, preferred_element_type=jnp.float32)]
    all_gather x2 -> x0, waiting for transfers between devices: 62.3 us -> none  [the longest x1 45.5 us: body(): lax.all_gather(out_grad, 'tensor', axis=0, tiled=True)]
    another operation x15 -> x0, other arithmetic: 36.2 us -> none  [the longest x9 19.6 us: solve_rows(): lower = jnp.linalg.cholesky(gram + jnp.diag(unused))]
    another operation x3 -> x0, matrix products: 5.13 us -> none  [solve_rows(): lax.linalg.triangular_solve(lower, ptrans, left_side=True, lower=True)]
  transfers between devices with their start and end apart: 4 -> 0, of which waited for: 4 -> 0; matrix products, arithmetic and copies ran while one was open for 10% -> 0% of each run, Pallas kernels for 0% -> 0%
where the time goes in v1:
time: 154 us
  Pallas kernels  142 us (92%)
  other arithmetic  6.42 us (4%)
  local copies, waits for them, and re-layouts  3.73 us (2%)
    pallas_call x1, Pallas kernels, kernel_body(): pl.pallas_call(functools.partial(front_kernel, n), out_shape=[shape(total...  81.6 us
    pallas_call x2, Pallas kernels, dp_sum(): pl.pallas_call(sum_kernel, out_shape=[jax.ShapeDtypeStruct(a.shape, BF),...  45.4 us
    pallas_call x1, Pallas kernels, kernel_body(): pl.pallas_call(back_kernel, out_shape=[jax.ShapeDtypeStruct((1, RMAX, fea...  15.2 us
    unnamed x6, local copies, waits for them, and re-layouts  3.73 us

profile of v1, /device:TPU:0, one launch (start us, length us, event | category | flops | bytes accessed | tf_op | source)
XLA Modules:
  0.0 153.7 jit_solution(12264139202940286681)
XLA Ops:
  1.3 0.7 broadcast_subtract_fusion.unused_ref
  2.0 1.3 fusion.mask_ref
  3.3 1.9 %broadcast_select_fusion.g_hbm = bf16[64,4096]{1,0:T(8,128)(2,1)} fusion(bf16[64,4096]{1,0:T(8,128)(2,1)} %param.10, pred[64]{0:T(512)(128)(4,1)S(1)} %add_compare_fusion), kind=kLoop, calls=%fused_computation.1 | loop fusion | flops 262144 | bytes 1048640 | tf_op jit(solution)/shard_map/jit(_where)/select_n | solution.py:498
  5.3 81.6 %front.1 = (bf16[256,4096]{1,0:T(8,128)(2,1)}, bf16[256,4096]{1,0:T(8,128)(2,1)}, bf16[256,3584]{1,0:T(8,128)(2,1)}, bf16[256,3584]{1,0:T(8,128)(2,1)}, bf16[256...) custom-call(bf16[64,4096]{1,0:T(8,128)(2,1)} %x_hbm.1, ...), custom_call_target="tpu_custom_call" | custom-call | tf_op jit(solution)/shard_map/front/pallas_call | solution.py:509
  86.9 0.0 copy-start.1
  86.9 1.2 copy-done.1
  88.1 0.0 copy-start.2
  88.1 1.0 copy-done.2
  89.1 23.5 %dp_sum_1.1 = (bf16[128,4096]{1,0:T(8,128)(2,1)S(1)}, bf16[64,3584]{1,0:T(8,128)(2,1)S(1)}) custom-call(bf16[128,4096]{1,0:T(8,128)(2,1)S(1)} %copy-done.1, bf16[64,3584]{1,0:T(8,128)(2,1)S(1)} %copy-done.2), custom_call_target="tpu_custom_call" | custom-call | tf_op jit(solution)/shard_map/dp_sum_1/pallas_call | solution.py:379
  112.7 0.0 copy-start
  112.7 1.5 copy-done
  114.2 15.2 %back.1 = (f32[1,64,4096]{2,1,0:T(8,128)}, f32[1,64,4096]{2,1,0:T(8,128)}, f32[64,3584]{1,0:T(8,128)}, bf16[128,3584]{1,0:T(8,128)(2,1)S(1)}, bf16[64,4096]{1,0:T(8,128)(2,1)S(1)}) custom-call(bf16[128,4096]{1,0:T(8,128)(2,1)S(1)} %get-tuple-element.24.pa_ref, bf16[64,3584]{1,0:T(8,128)(2,1)S(1)} %get-tuple-element.25.pb_ref, ...), custom_call_target="tpu_custom_call" | custom-call | tf_op jit(solution)/shard_map/back/pallas_call | solution.py:536
  129.4 21.9 %dp_sum_2.1 = (bf16[128,3584]{1,0:T(8,128)(2,1)S(1)}, bf16[64,4096]{1,0:T(8,128)(2,1)S(1)}) custom-call(bf16[128,3584]{1,0:T(8,128)(2,1)S(1)} %get-tuple-element.32.a_ref, bf16[64,4096]{1,0:T(8,128)(2,1)S(1)} %get-tuple-element.33.b_ref), custom_call_target="tpu_custom_call" | custom-call | tf_op jit(solution)/shard_map/dp_sum_2/pallas_call | solution.py:379
  151.2 1.4 slice_convert_fusion
  152.6 1.0 bitcast_convert_fusion
  (1 shorter events, 0.0 us)
Async XLA Ops:
  86.9 1.2 copy-start.1
  88.1 1.0 copy-start.2
  112.7 1.5 copy-start

commit v2 on v1

--- a/solution.py
+++ b/solution.py
@@ -115,10 +115,11 @@
 
 
 def front_kernel(
-    n, x_hbm, g_hbm, gate_hbm, up_hbm, w_hbm, bw_ref, bm_ref, mask_ref,
-    x_full, g_full, hid, d_gate, d_up, pt_a, pt_b,
+    n, x_hbm, g_mine, gate_hbm, up_hbm, w_hbm, bw_ref, bm_ref, ranks_ref, count_ref,
+    x_out, g_out, hid_out, d_gate_out, d_up_out, pt_a, pt_b,
+    x_full, g_full, hid, d_gate, d_up,
     w_vmem, gate_v, up_v, acc, proj_a, proj_b,
-    load_sem, w_sem, own_sem, send_sem, recv_sem,
+    load_sem, w_sem, own_sem, store_sem, send_sem, recv_sem,
 ):
     me = lax.axis_index("tensor")
     rows = x_hbm.shape[0]
@@ -132,10 +133,14 @@
         )
         for i in range(tiles)
     ]
-    own = []
-    for a, (hbm, full) in enumerate(((g_hbm, g_full), (x_hbm, x_full))):
-        mine = pl.ds(pl.multiple_of(me * rows, rows), rows)
-        own.append(pltpu.make_async_copy(hbm, full.at[mine], own_sem.at[a]))
+    mine = pl.ds(pl.multiple_of(me * rows, rows), rows)
+    own = [pltpu.make_async_copy(x_hbm, x_full.at[mine], own_sem.at[0])]
+    stores = [
+        pltpu.make_async_copy(src, dst, store_sem.at[i])
+        for i, (src, dst) in enumerate(
+            ((g_full, g_out), (hid, hid_out), (d_gate, d_gate_out), (d_up, d_up_out), (x_full, x_out))
+        )
+    ]
     loads = [
         pltpu.make_async_copy(gate_hbm, gate_v, load_sem.at[0]),
         pltpu.make_async_copy(up_hbm, up_v, load_sem.at[1]),
@@ -151,6 +156,10 @@
     def _():
         pl.semaphore_signal(barrier, inc=1, device_id={"tensor": me + 1}, device_id_type=MESH)
 
+    row = me * rows + lax.broadcasted_iota(jnp.int32, g_mine.shape, 0)
+    g_full[mine, :] = jnp.where(row < count_ref[0], g_mine[...].astype(F32), 0.0).astype(BF)
+    rank_col = lax.broadcasted_iota(jnp.int32, (1, RMAX), 1)
+    masks = [jnp.where(rank_col < ranks_ref[k], 1.0, 0.0).astype(F32) for k in range(3)]
     inside = jnp.logical_and(me > 0, me < n - 1)
 
     @pl.when(inside)
@@ -162,13 +171,12 @@
         pl.semaphore_wait(barrier, 1)
 
     fulls = (g_full, x_full)
-    hbms = (g_hbm, x_hbm)
 
     def copy(a, side, shard, piece, first):
         place = fulls[a].at[pl.ds(pl.multiple_of(shard * rows + piece * CHUNK, CHUNK), CHUNK)]
         source = place
-        if first:
-            source = hbms[a].at[pl.ds(pl.multiple_of(piece * CHUNK, CHUNK), CHUNK)]
+        if first and a == 1:
+            source = x_hbm.at[pl.ds(pl.multiple_of(piece * CHUNK, CHUNK), CHUNK)]
         return pltpu.make_async_remote_copy(
             src_ref=source,
             dst_ref=place,
@@ -224,7 +232,8 @@
     for item in own + loads + w_loads:
         item.wait()
 
-    proj_b[...] = (dot(g_full[...], bm_ref[...], (1, 0)) * mask_ref[2:3, :]).astype(BF)
+    stores[0].start()
+    proj_b[...] = (dot(g_full[...], bm_ref[...], (1, 0)) * masks[2]).astype(BF)
     acc[...] = jnp.zeros_like(acc)
 
     def tile(i, carry):
@@ -253,11 +262,14 @@
         return carry
 
     lax.fori_loop(0, tiles, tile, 0)
+    for item in stores[1:4]:
+        item.start()
     for d in range(2, n):
         each_piece(1, d)
+    stores[4].start()
 
     for k in range(2):
-        proj_a[k] = (acc[k] * mask_ref[k:k + 1, :]).astype(BF)
+        proj_a[k] = (acc[k] * masks[k]).astype(BF)
 
     def left(i, carry):
         cols = columns(i, TILE)
@@ -282,6 +294,8 @@
                 return carry
 
             lax.fori_loop(0, pieces, drain, 0)
+    for item in stores:
+        item.wait()
 
 
 def sum_kernel(
@@ -420,7 +434,7 @@
 
 
 def back_kernel(
-    pa_ref, pb_ref, unused_ref, x_hbm, g_hbm, hid_hbm, dg_hbm, du_hbm,
+    pa_ref, pb_ref, ranks_ref, x_hbm, g_hbm, hid_hbm, dg_hbm, du_hbm,
     p_gate, p_up, p_down, qa, qb,
     x_v, g_v, hid_v, dg_v, du_v, pha, phb, split, sem,
 ):
@@ -440,7 +454,7 @@
     both = dot(pa_ref[...], pa_ref[...], (1, 1))
     grams = [both[:size, :size], both[size:, size:], dot(pb_ref[...], pb_ref[...], (1, 1))]
     for k in range(3):
-        grams[k] = grams[k] + jnp.where(row == col, unused_ref[k:k + 1, :], 0.0)
+        grams[k] = grams[k] + jnp.where(jnp.logical_and(row == col, col >= ranks_ref[k]), 1.0, 0.0)
     for k, inverse in enumerate(inverse_factors(grams)):
         high = inverse.astype(BF)
         split[k, 0] = high
@@ -494,14 +508,10 @@
     total = rows * n
     tiles = width // TILE
     pieces = rows // CHUNK
-    here = lax.axis_index("tensor") * rows + jnp.arange(rows, dtype=jnp.int32)
-    masked = jnp.where((here < token_count[0])[:, None], out_grad, jnp.zeros_like(out_grad))
-    used = jnp.arange(RMAX)[None, :] < ranks[:, None]
-    mask = used.astype(F32)
-    unused = 1.0 - mask
     dma = pltpu.SemaphoreType.DMA
     vmem = pl.BlockSpec(memory_space=pltpu.VMEM)
     hbm = pl.BlockSpec(memory_space=pl.ANY)
+    smem = pl.BlockSpec(memory_space=pltpu.SMEM)
 
     def shape(*dims):
         return jax.ShapeDtypeStruct(dims, BF)
@@ -512,24 +522,27 @@
             shape(total, features), shape(total, features), shape(total, width),
             shape(total, width), shape(total, width), shape(2 * RMAX, features), shape(RMAX, width),
         ],
-        in_specs=[hbm] * 5 + [vmem] * 3,
-        out_specs=[vmem] * 7,
+        in_specs=[hbm, vmem] + [hbm] * 3 + [vmem] * 2 + [smem] * 2,
+        out_specs=[hbm] * 5 + [vmem] * 2,
         scratch_shapes=[
+            pltpu.VMEM((total, features), BF), pltpu.VMEM((total, features), BF),
+            pltpu.VMEM((total, width), BF), pltpu.VMEM((total, width), BF),
+            pltpu.VMEM((total, width), BF),
             pltpu.VMEM((width, features), BF),
             pltpu.VMEM((total, width), BF),
             pltpu.VMEM((total, width), BF),
             pltpu.VMEM((2, total, RMAX), F32),
             pltpu.VMEM((2, total, RMAX), BF),
             pltpu.VMEM((total, RMAX), BF),
-            dma((2,)), dma((tiles,)), dma((2,)),
+            dma((2,)), dma((tiles,)), dma((1,)), dma((5,)),
             dma((2, 2, n, pieces)), dma((2, n, pieces)),
         ],
         compiler_params=pltpu.CompilerParams(
             collective_id=0, has_side_effects=True, vmem_limit_bytes=60 * MIB
         ),
         name="front",
-    )(inputs, masked, gate_act, up_act, w_down, jnp.asarray(table_of(width)),
-      jnp.asarray(table_of(features)), mask)
+    )(inputs, out_grad, gate_act, up_act, w_down, jnp.asarray(table_of(width)),
+      jnp.asarray(table_of(features)), ranks, token_count)
 
     sum_a, sum_b = dp_sum(pt_a, pt_b, 1)
 
@@ -541,7 +554,7 @@
             jax.ShapeDtypeStruct((RMAX, width), F32),
             shape(2 * RMAX, width), shape(RMAX, features),
         ],
-        in_specs=[vmem] * 3 + [hbm] * 5,
+        in_specs=[vmem] * 2 + [smem] + [hbm] * 5,
         out_specs=[vmem] * 5,
         scratch_shapes=[
             pltpu.VMEM((total, features), BF), pltpu.VMEM((total, features), BF),
@@ -553,7 +566,7 @@
         ],
         compiler_params=pltpu.CompilerParams(vmem_limit_bytes=48 * MIB),
         name="back",
-    )(sum_a, sum_b, unused, x_full, g_full, hid, d_gate, d_up)
+    )(sum_a, sum_b, ranks, x_full, g_full, hid, d_gate, d_up)
 
     qa, qb = dp_sum(qa, qb, 2)
     return (

time: 154 us -> 147 us (0.955)
  other arithmetic: 6.42 us -> 2.45 us
  Pallas kernels: 142 us -> 140 us
    pallas_call x1, Pallas kernels: 81.6 us -> 78.5 us  [kernel_body(): pl.pallas_call(functools.partial(front_kernel, n), out_shape=[shape(total...]
    select_n x1 -> x0, other arithmetic: 1.94 us -> none  [kernel_body(): jnp.where((here < token_count[0])[:, None], out_grad, jnp.zeros_like(out_...]
    unnamed x6 -> x8, local copies, waits for them, and re-layouts: 3.73 us -> 3.73 us
where the time goes in v2:
time: 147 us
  Pallas kernels  140 us (95%)
  local copies, waits for them, and re-layouts  3.73 us (3%)
  other arithmetic  2.45 us (2%)
    pallas_call x1, Pallas kernels, kernel_body(): pl.pallas_call(functools.partial(front_kernel, n), out_shape=[shape(total...  78.5 us
    pallas_call x2, Pallas kernels, dp_sum(): pl.pallas_call(sum_kernel, out_shape=[jax.ShapeDtypeStruct(a.shape, BF),...  45.4 us
    pallas_call x1, Pallas kernels, kernel_body(): pl.pallas_call(back_kernel, out_shape=[jax.ShapeDtypeStruct((1, RMAX, fea...  15.7 us
    unnamed x8, local copies, waits for them, and re-layouts  3.73 us

profile of v2, /device:TPU:0, one launch (start us, length us, event | category | flops | bytes accessed | tf_op | source)
XLA Modules:
  0.0 147.2 jit_solution(1863063000160858557)
XLA Ops:
  1.3 0.0 copy-start.3
  1.3 78.5 %front.1 = (bf16[256,4096]{1,0:T(8,128)(2,1)}, bf16[256,4096]{1,0:T(8,128)(2,1)}, bf16[256,3584]{1,0:T(8,128)(2,1)}, bf16[256,3584]{1,0:T(8,128)(2,1)}, bf16[256...) custom-call(bf16[64,4096]{1,0:T(8,128)(2,1)} %x_hbm.1, bf16[64,4096]{1,0:T(8,128)(2,1)} %g_mine.1, ...), custom_call_target="tpu_custom_call" | custom-call | tf_op jit(solution)/shard_map/front/pallas_call | solution.py:519
  79.8 0.0 copy-start.1
  79.8 1.2 copy-done.1
  81.1 0.0 copy-start.2
  81.1 1.0 copy-done.2
  82.1 23.5 %dp_sum_1.1 = (bf16[128,4096]{1,0:T(8,128)(2,1)S(1)}, bf16[64,3584]{1,0:T(8,128)(2,1)S(1)}) custom-call(bf16[128,4096]{1,0:T(8,128)(2,1)S(1)} %copy-done.1, bf16[64,3584]{1,0:T(8,128)(2,1)S(1)} %copy-done.2), custom_call_target="tpu_custom_call" | custom-call | tf_op jit(solution)/shard_map/dp_sum_1/pallas_call | solution.py:393
  105.6 0.0 copy-done.3
  105.6 0.0 copy-start
  105.7 1.5 %copy-done = bf16[256,3584]{1,0:T(8,128)(2,1)S(1)} copy-done((bf16[256,3584]{1,0:T(8,128)(2,1)S(1)}, bf16[256,3584]{1,0:T(8,128)(2,1)}, u32[]{:S(2)}) %copy-start) | copy-done | bytes 1835032
  107.1 15.7 %back.1 = (f32[1,64,4096]{2,1,0:T(8,128)}, f32[1,64,4096]{2,1,0:T(8,128)}, f32[64,3584]{1,0:T(8,128)}, bf16[128,3584]{1,0:T(8,128)(2,1)S(1)}, bf16[64,4096]{1,0:T(8,128)(2,1)S(1)}) custom-call(bf16[128,4096]{1,0:T(8,128)(2,1)S(1)} %get-tuple-element.24.pa_ref, bf16[64,3584]{1,0:T(8,128)(2,1)S(1)} %get-tuple-element.25.pb_ref, s32[3]{0:T(128)S(1)} %copy-done.3, ...), custom_call_target="tpu_custom_call" | custom-call | tf_op jit(solution)/shard_map/back/pallas_call | solution.py:549
  122.9 21.9 %dp_sum_2.1 = (bf16[128,3584]{1,0:T(8,128)(2,1)S(1)}, bf16[64,4096]{1,0:T(8,128)(2,1)S(1)}) custom-call(bf16[128,3584]{1,0:T(8,128)(2,1)S(1)} %get-tuple-element.32.a_ref, bf16[64,4096]{1,0:T(8,128)(2,1)S(1)} %get-tuple-element.33.b_ref), custom_call_target="tpu_custom_call" | custom-call | tf_op jit(solution)/shard_map/dp_sum_2/pallas_call | solution.py:393
  144.7 1.4 slice_convert_fusion
  146.1 1.0 bitcast_convert_fusion
Async XLA Ops:
  1.3 104.4 %copy-start.3 = (s32[3]{0:T(128)S(1)}, s32[3]{0:T(128)}, u32[]{:S(2)}) copy-start(s32[3]{0:T(128)} %ranks_ref.3) | copy-start | bytes 40
  79.8 1.2 copy-start.1
  81.1 1.0 copy-start.2
  105.6 1.5 %copy-start = (bf16[256,3584]{1,0:T(8,128)(2,1)S(1)}, bf16[256,3584]{1,0:T(8,128)(2,1)}, u32[]{:S(2)}) copy-start(bf16[256,3584]{1,0:T(8,128)(2,1)} %get-tuple-element.28.hid_hbm) | copy-start | bytes 5505028

commit v3 on v2

--- a/solution.py
+++ b/solution.py
@@ -116,10 +116,10 @@
 
 def front_kernel(
     n, x_hbm, g_mine, gate_hbm, up_hbm, w_hbm, bw_ref, bm_ref, ranks_ref, count_ref,
-    x_out, g_out, hid_out, d_gate_out, d_up_out, pt_a, pt_b,
+    x_out, g_out, hid_out, d_gate_out, d_up_out, pt_a, sum_b,
     x_full, g_full, hid, d_gate, d_up,
-    w_vmem, gate_v, up_v, acc, proj_a, proj_b,
-    load_sem, w_sem, own_sem, store_sem, send_sem, recv_sem,
+    w_vmem, gate_v, up_v, acc, proj_a, proj_b, pt_b,
+    load_sem, w_sem, own_sem, store_sem, send_sem, recv_sem, *sum_refs,
 ):
     me = lax.axis_index("tensor")
     rows = x_hbm.shape[0]
@@ -146,7 +146,10 @@
         pltpu.make_async_copy(up_hbm, up_v, load_sem.at[1]),
     ]
 
+    down = DpSum(pt_b, sum_b, *sum_refs)
     barrier = pltpu.get_barrier_semaphore()
+    for peer in down.peers():
+        pl.semaphore_signal(barrier, inc=1, device_id={"dp": peer}, device_id_type=MESH)
 
     @pl.when(me > 0)
     def _():
@@ -164,11 +167,11 @@
 
     @pl.when(inside)
     def _():
-        pl.semaphore_wait(barrier, 2)
+        pl.semaphore_wait(barrier, 6)
 
     @pl.when(jnp.logical_not(inside))
     def _():
-        pl.semaphore_wait(barrier, 1)
+        pl.semaphore_wait(barrier, 5)
 
     fulls = (g_full, x_full)
 
@@ -264,8 +267,12 @@
     lax.fori_loop(0, tiles, tile, 0)
     for item in stores[1:4]:
         item.start()
-    for d in range(2, n):
-        each_piece(1, d)
+    down.start_pair()
+    each_piece(1, n - 2)
+    down.start_scatter()
+    down.start_gather()
+    down.start_hand()
+    each_piece(1, n - 1)
     stores[4].start()
 
     for k in range(2):
@@ -296,115 +303,134 @@
             lax.fori_loop(0, pieces, drain, 0)
     for item in stores:
         item.wait()
-
-
-def sum_kernel(
-    a_ref, b_ref, oa_ref, ob_ref, sib_a, sib_b, mid_a, mid_b, got_a, got_b,
-    pair_send, pair_recv, rs_send, rs_recv, ag_send, ag_recv, out_send, out_recv,
-):
-    me = lax.axis_index("dp")
-    core = lax.rem(me, 2)
-    chip = me // 2
-    sibling = chip * 2 + 1 - core
-    others = (3 - chip, chip + 1 - 2 * lax.rem(chip, 2), lax.rem(chip + 2, 4))
-
-    barrier = pltpu.get_barrier_semaphore()
-    pl.semaphore_signal(barrier, inc=1, device_id={"dp": sibling}, device_id_type=MESH)
-    for other in others:
-        pl.semaphore_signal(barrier, inc=1, device_id={"dp": other * 2 + core}, device_id_type=MESH)
-    pl.semaphore_wait(barrier, 4)
-
-    def remote(src, dst, send, recv, device):
+    down.finish()
+
+
+class DpSum:
+    def __init__(self, src, out, sib, mid, got, pair, scatter, gather, hand):
+        me = lax.axis_index("dp")
+        self.core = lax.rem(me, 2)
+        self.chip = me // 2
+        self.sibling = self.chip * 2 + 1 - self.core
+        self.others = (
+            3 - self.chip, self.chip + 1 - 2 * lax.rem(self.chip, 2), lax.rem(self.chip + 2, 4)
+        )
+        self.src, self.out, self.sib, self.mid, self.got = src, out, sib, mid, got
+        self.sems = (pair, scatter, gather, hand)
+        self.half = src.shape[1] // 2
+        self.part = src.shape[0] // 4
+        self.cols = columns(self.core, self.half)
+
+    def peers(self):
+        return [self.sibling] + [other * 2 + self.core for other in self.others]
+
+    def rows(self, chip):
+        return pl.ds(pl.multiple_of(chip * self.part, self.part), self.part)
+
+    def remote(self, src, dst, stage, index, device):
+        sems = self.sems[stage]
         return pltpu.make_async_remote_copy(
-            src_ref=src, dst_ref=dst, send_sem=send, recv_sem=recv,
+            src_ref=src, dst_ref=dst, send_sem=sems.at[0, index], recv_sem=sems.at[1, index],
             device_id={"dp": device}, device_id_type=MESH,
         )
 
-    arrays = (
-        (a_ref, oa_ref, sib_a, mid_a, got_a),
-        (b_ref, ob_ref, sib_b, mid_b, got_b),
-    )
-    started = []
-    pairs = []
-    for n, (src, out, sib, mid, got) in enumerate(arrays):
-        half = src.shape[1] // 2
-        item = remote(src.at[:, columns(1 - core, half)], sib, pair_send.at[n], pair_recv.at[n], sibling)
+    def start_pair(self):
+        self.pair = self.remote(
+            self.src.at[:, columns(1 - self.core, self.half)], self.sib, 0, 0, self.sibling
+        )
+        self.pair.start()
+
+    def start_scatter(self):
+        self.pair.wait_recv()
+        both = self.src[:, self.cols].astype(F32) + self.sib[...].astype(F32)
+        self.mid[...] = both.astype(BF)
+        self.scattered = []
+        for k, other in enumerate(self.others):
+            item = self.remote(
+                self.mid.at[self.rows(other)], self.got.at[k], 1, k, other * 2 + self.core
+            )
+            item.start()
+            self.scattered.append(item)
+
+    def start_gather(self):
+        rows = self.rows(self.chip)
+        total = self.src[rows, self.cols].astype(F32) + self.sib[rows, :].astype(F32)
+        for k in range(3):
+            self.scattered[k].wait_recv()
+            total = total + self.got[k].astype(F32)
+        self.out[rows, self.cols] = total.astype(BF)
+        block = self.out.at[rows, self.cols]
+        self.gathered = []
+        for k, other in enumerate(self.others):
+            item = self.remote(block, block, 2, k, other * 2 + self.core)
+            item.start()
+            self.gathered.append(item)
+        item = self.remote(block, block, 3, 3, self.sibling)
         item.start()
-        pairs.append(item)
-        started.append(item)
-    scattered = []
-    for n, (src, out, sib, mid, got) in enumerate(arrays):
-        half = src.shape[1] // 2
-        part = src.shape[0] // 4
-        pairs[n].wait_recv()
-        mid[...] = (src[:, columns(core, half)].astype(F32) + sib[...].astype(F32)).astype(BF)
-        for k, other in enumerate(others):
-            rows = pl.ds(pl.multiple_of(other * part, part), part)
-            item = remote(mid.at[rows], got.at[k], rs_send.at[n, k], rs_recv.at[n, k], other * 2 + core)
+        self.handed = [item]
+
+    def start_hand(self):
+        for k in (1, 2, 0):
+            self.gathered[k].wait_recv()
+            block = self.out.at[self.rows(self.others[k]), self.cols]
+            item = self.remote(block, block, 3, k, self.sibling)
             item.start()
-            scattered.append(item)
-            started.append(item)
-    gathered = []
-    handed = []
-    for n, (src, out, sib, mid, got) in enumerate(arrays):
-        half = src.shape[1] // 2
-        part = src.shape[0] // 4
-        rows = pl.ds(pl.multiple_of(chip * part, part), part)
-        cols = columns(core, half)
-        total = src[rows, cols].astype(F32) + sib[rows, :].astype(F32)
-        for k in range(3):
-            scattered[3 * n + k].wait_recv()
-            total = total + got[k].astype(F32)
-        out[rows, cols] = total.astype(BF)
-        block = out.at[rows, cols]
-        for k, other in enumerate(others):
-            item = remote(block, block, ag_send.at[n, k], ag_recv.at[n, k], other * 2 + core)
-            item.start()
-            gathered.append(item)
-            started.append(item)
-        item = remote(block, block, out_send.at[n, 3], out_recv.at[n, 3], sibling)
-        item.start()
-        handed.append(item)
-        started.append(item)
-    for n, (src, out, sib, mid, got) in enumerate(arrays):
-        half = src.shape[1] // 2
-        part = src.shape[0] // 4
-        for k in (1, 2, 0):
-            gathered[3 * n + k].wait_recv()
-            block = out.at[pl.ds(pl.multiple_of(others[k] * part, part), part), columns(core, half)]
-            item = remote(block, block, out_send.at[n, k], out_recv.at[n, k], sibling)
-            item.start()
-            handed.append(item)
-            started.append(item)
-    for item in handed:
-        item.wait_recv()
-    for item in started:
-        item.wait_send()
-
-
-def dp_sum(a, b, number):
-    def half(array):
-        return pltpu.VMEM((array.shape[0], array.shape[1] // 2), BF)
-
-    def got(array):
-        return pltpu.VMEM((3, array.shape[0] // 4, array.shape[1] // 2), BF)
-
+            self.handed.append(item)
+
+    def finish(self):
+        for item in self.handed:
+            item.wait_recv()
+        for item in [self.pair] + self.scattered + self.gathered + self.handed:
+            item.wait_send()
+
+
+def sum_scratch(rows, cols):
     dma = pltpu.SemaphoreType.DMA
+    return [
+        pltpu.VMEM((rows, cols // 2), BF), pltpu.VMEM((rows, cols // 2), BF),
+        pltpu.VMEM((3, rows // 4, cols // 2), BF),
+        dma((2, 1)), dma((2, 3)), dma((2, 3)), dma((2, 4)),
+    ]
+
+
+def sum_kernel(count, *refs):
+    sums = [
+        DpSum(refs[n], refs[count + n], *refs[2 * count + 7 * n:2 * count + 7 * n + 7])
+        for n in range(count)
+    ]
+    barrier = pltpu.get_barrier_semaphore()
+    peers = sums[0].peers()
+    for peer in peers:
+        pl.semaphore_signal(barrier, inc=1, device_id={"dp": peer}, device_id_type=MESH)
+    pl.semaphore_wait(barrier, len(peers))
+    for item in sums:
+        item.start_pair()
+    for item in sums:
+        item.start_scatter()
+    for item in sums:
+        item.start_gather()
+    for item in sums:
+        item.start_hand()
+    for item in sums:
+        item.finish()
+
+
+def dp_sum(number, *arrays):
+    count = len(arrays)
+    scratch = []
+    for array in arrays:
+        scratch += sum_scratch(*array.shape)
     return pl.pallas_call(
-        sum_kernel,
-        out_shape=[jax.ShapeDtypeStruct(a.shape, BF), jax.ShapeDtypeStruct(b.shape, BF)],
-        in_specs=[pl.BlockSpec(memory_space=pltpu.VMEM)] * 2,
-        out_specs=[pl.BlockSpec(memory_space=pltpu.VMEM)] * 2,
-        scratch_shapes=[
-            half(a), half(b), half(a), half(b), got(a), got(b),
-            dma((2,)), dma((2,)), dma((2, 3)), dma((2, 3)), dma((2, 3)), dma((2, 3)),
-            dma((2, 4)), dma((2, 4)),
-        ],
+        functools.partial(sum_kernel, count),
+        out_shape=[jax.ShapeDtypeStruct(array.shape, BF) for array in arrays],
+        in_specs=[pl.BlockSpec(memory_space=pltpu.VMEM)] * count,
+        out_specs=[pl.BlockSpec(memory_space=pltpu.VMEM)] * count,
+        scratch_shapes=scratch,
         compiler_params=pltpu.CompilerParams(
             collective_id=number, has_side_effects=True, vmem_limit_bytes=32 * MIB
         ),
         name="dp_sum_%d" % number,
-    )(a, b)
+    )(*arrays)
 
 
 def inverse_factors(grams):
@@ -516,7 +542,7 @@
     def shape(*dims):
         return jax.ShapeDtypeStruct(dims, BF)
 
-    x_full, g_full, hid, d_gate, d_up, pt_a, pt_b = pl.pallas_call(
+    x_full, g_full, hid, d_gate, d_up, pt_a, sum_b = pl.pallas_call(
         functools.partial(front_kernel, n),
         out_shape=[
             shape(total, features), shape(total, features), shape(total, width),
@@ -534,9 +560,10 @@
             pltpu.VMEM((2, total, RMAX), F32),
             pltpu.VMEM((2, total, RMAX), BF),
             pltpu.VMEM((total, RMAX), BF),
+            pltpu.VMEM((RMAX, width), BF),
             dma((2,)), dma((tiles,)), dma((1,)), dma((5,)),
             dma((2, 2, n, pieces)), dma((2, n, pieces)),
-        ],
+        ] + sum_scratch(RMAX, width),
         compiler_params=pltpu.CompilerParams(
             collective_id=0, has_side_effects=True, vmem_limit_bytes=60 * MIB
         ),
@@ -544,7 +571,7 @@
     )(inputs, out_grad, gate_act, up_act, w_down, jnp.asarray(table_of(width)),
       jnp.asarray(table_of(features)), ranks, token_count)
 
-    sum_a, sum_b = dp_sum(pt_a, pt_b, 1)
+    sum_a, = dp_sum(1, pt_a)
 
     p_gate, p_up, p_down, qa, qb = pl.pallas_call(
         back_kernel,
@@ -568,7 +595,7 @@
         name="back",
     )(sum_a, sum_b, ranks, x_full, g_full, hid, d_gate, d_up)
 
-    qa, qb = dp_sum(qa, qb, 2)
+    qa, qb = dp_sum(2, qa, qb)
     return (
         p_gate, qa[:RMAX].astype(F32), p_up, qa[RMAX:].astype(F32), p_down, qb.astype(F32)[None],
     )

time: 147 us -> 143 us (0.973)
  Pallas kernels: 140 us -> 137 us
    pallas_call x2, Pallas kernels: 45.4 us -> 41.4 us  [dp_sum(): pl.pallas_call(functools.partial(sum_kernel, count), out_shape=[jax.Shape...]
where the time goes in v3:
time: 143 us
  Pallas kernels  137 us (96%)
  other arithmetic  2.45 us (2%)
  local copies, waits for them, and re-layouts  2.37 us (2%)
    pallas_call x1, Pallas kernels, kernel_body(): pl.pallas_call(functools.partial(front_kernel, n), out_shape=[shape(total...  79.7 us
    pallas_call x2, Pallas kernels, dp_sum(): pl.pallas_call(functools.partial(sum_kernel, count), out_shape=[jax.Shape...  41.4 us
    pallas_call x1, Pallas kernels, kernel_body(): pl.pallas_call(back_kernel, out_shape=[jax.ShapeDtypeStruct((1, RMAX, fea...  15.7 us

profile of v3, /device:TPU:0, one launch (start us, length us, event | category | flops | bytes accessed | tf_op | source)
XLA Modules:
  0.0 142.9 jit_solution(11140633562164479856)
XLA Ops:
  1.3 0.0 copy-start.3
  1.3 79.7 %front.1 = (bf16[256,4096]{1,0:T(8,128)(2,1)}, bf16[256,4096]{1,0:T(8,128)(2,1)}, bf16[256,3584]{1,0:T(8,128)(2,1)}, bf16[256,3584]{1,0:T(8,128)(2,1)}, bf16[256...) custom-call(bf16[64,4096]{1,0:T(8,128)(2,1)} %x_hbm.1, bf16[64,4096]{1,0:T(8,128)(2,1)} %g_mine.1, ...), custom_call_target="tpu_custom_call" | custom-call | tf_op jit(solution)/shard_map/front/pallas_call | solution.py:545
  81.0 0.0 copy-start
  81.0 0.0 copy-start.1
  81.0 1.3 copy-done.1
  82.3 19.5 %dp_sum_1.1.pa_ref = bf16[128,4096]{1,0:T(8,128)(2,1)S(1)} custom-call(bf16[128,4096]{1,0:T(8,128)(2,1)S(1)} %copy-done.1), custom_call_target="tpu_custom_call" | custom-call | tf_op jit(solution)/shard_map/dp_sum_1/pallas_call | solution.py:423
  101.8 0.0 copy-done.3
  101.8 0.0 copy-done
  101.8 0.0 copy-start.2
  101.8 1.0 copy-done.2
  102.9 15.7 %back.1 = (f32[1,64,4096]{2,1,0:T(8,128)}, f32[1,64,4096]{2,1,0:T(8,128)}, f32[64,3584]{1,0:T(8,128)}, bf16[128,3584]{1,0:T(8,128)(2,1)S(1)}, bf16[64,4096]{1,0:T(8,128)(2,1)S(1)}) custom-call(bf16[128,4096]{1,0:T(8,128)(2,1)S(1)} %dp_sum_1.1.pa_ref, bf16[64,3584]{1,0:T(8,128)(2,1)S(1)} %copy-done.2, s32[3]{0:T(128)S(1)} %copy-done.3, ...), custom_call_target="tpu_custom_call" | custom-call | tf_op jit(solution)/shard_map/back/pallas_call | solution.py:576
  118.6 21.9 %dp_sum_2.1 = (bf16[128,3584]{1,0:T(8,128)(2,1)S(1)}, bf16[64,4096]{1,0:T(8,128)(2,1)S(1)}) custom-call(bf16[128,3584]{1,0:T(8,128)(2,1)S(1)} %get-tuple-element.28.refs_0_, bf16[64,4096]{1,0:T(8,128)(2,1)S(1)} %get-tuple-element.29.refs_1_), custom_call_target="tpu_custom_call" | custom-call | tf_op jit(solution)/shard_map/dp_sum_2/pallas_call | solution.py:423
  140.5 1.4 slice_convert_fusion
  141.9 1.0 bitcast_convert_fusion
Async XLA Ops:
  1.3 100.5 %copy-start.3 = (s32[3]{0:T(128)S(1)}, s32[3]{0:T(128)}, u32[]{:S(2)}) copy-start(s32[3]{0:T(128)} %ranks_ref.3) | copy-start | bytes 40
  81.0 20.9 %copy-start = (bf16[256,3584]{1,0:T(8,128)(2,1)S(1)}, bf16[256,3584]{1,0:T(8,128)(2,1)}, u32[]{:S(2)}) copy-start(bf16[256,3584]{1,0:T(8,128)(2,1)} %get-tuple-element.24.hid_hbm) | copy-start | bytes 5505028
  81.0 1.4 copy-start.1
  101.8 1.0 copy-start.2

commit v4 on v3

--- a/solution.py
+++ b/solution.py
@@ -394,10 +394,12 @@
 
 
 def sum_kernel(count, *refs):
-    sums = [
-        DpSum(refs[n], refs[count + n], *refs[2 * count + 7 * n:2 * count + 7 * n + 7])
-        for n in range(count)
-    ]
+    sums = []
+    for n in range(count):
+        for first in range(0, refs[n].shape[0], RMAX):
+            own = 2 * count + 7 * len(sums)
+            taken = pl.ds(first, RMAX)
+            sums.append(DpSum(refs[n].at[taken], refs[count + n].at[taken], *refs[own:own + 7]))
     barrier = pltpu.get_barrier_semaphore()
     peers = sums[0].peers()
     for peer in peers:
@@ -419,7 +421,7 @@
     count = len(arrays)
     scratch = []
     for array in arrays:
-        scratch += sum_scratch(*array.shape)
+        scratch += (array.shape[0] // RMAX) * sum_scratch(RMAX, array.shape[1])
     return pl.pallas_call(
         functools.partial(sum_kernel, count),
         out_shape=[jax.ShapeDtypeStruct(array.shape, BF) for array in arrays],

time: 143 us -> 141 us (0.986)
  Pallas kernels: 137 us -> 134 us
    pallas_call x2, Pallas kernels: 41.4 us -> 38.9 us  [dp_sum(): pl.pallas_call(functools.partial(sum_kernel, count), out_shape=[jax.Shape...]
where the time goes in v4:
time: 141 us; the launch traced here: 140 us
  Pallas kernels  134 us (95%)
  other arithmetic  2.45 us (2%)
  local copies, waits for them, and re-layouts  2.37 us (2%)
    pallas_call x1, Pallas kernels, kernel_body(): pl.pallas_call(functools.partial(front_kernel, n), out_shape=[shape(total...  79.7 us
    pallas_call x2, Pallas kernels, dp_sum(): pl.pallas_call(functools.partial(sum_kernel, count), out_shape=[jax.Shape...  38.9 us
    pallas_call x1, Pallas kernels, kernel_body(): pl.pallas_call(back_kernel, out_shape=[jax.ShapeDtypeStruct((1, RMAX, fea...  15.7 us

profile of v4, /device:TPU:0, one launch (start us, length us, event | category | flops | bytes accessed | tf_op | source)
XLA Modules:
  0.0 140.5 jit_solution(7239472978570723837)
XLA Ops:
  1.3 0.0 copy-start.3
  1.3 79.7 %front.1 = (bf16[256,4096]{1,0:T(8,128)(2,1)}, bf16[256,4096]{1,0:T(8,128)(2,1)}, bf16[256,3584]{1,0:T(8,128)(2,1)}, bf16[256,3584]{1,0:T(8,128)(2,1)}, bf16[256...) custom-call(bf16[64,4096]{1,0:T(8,128)(2,1)} %x_hbm.1, bf16[64,4096]{1,0:T(8,128)(2,1)} %g_mine.1, ...), custom_call_target="tpu_custom_call" | custom-call | tf_op jit(solution)/shard_map/front/pallas_call | solution.py:547
  81.0 0.0 copy-start
  81.0 0.0 copy-start.1
  81.0 1.3 copy-done.1
  82.3 17.0 %dp_sum_1.1.pa_ref = bf16[128,4096]{1,0:T(8,128)(2,1)S(1)} custom-call(bf16[128,4096]{1,0:T(8,128)(2,1)S(1)} %copy-done.1), custom_call_target="tpu_custom_call" | custom-call | tf_op jit(solution)/shard_map/dp_sum_1/pallas_call | solution.py:425
  99.3 0.0 copy-done.3
  99.3 0.0 copy-done
  99.3 0.0 copy-start.2
  99.4 1.0 copy-done.2
  100.4 15.7 %back.1 = (f32[1,64,4096]{2,1,0:T(8,128)}, f32[1,64,4096]{2,1,0:T(8,128)}, f32[64,3584]{1,0:T(8,128)}, bf16[128,3584]{1,0:T(8,128)(2,1)S(1)}, bf16[64,4096]{1,0:T(8,128)(2,1)S(1)}) custom-call(bf16[128,4096]{1,0:T(8,128)(2,1)S(1)} %dp_sum_1.1.pa_ref, bf16[64,3584]{1,0:T(8,128)(2,1)S(1)} %copy-done.2, s32[3]{0:T(128)S(1)} %copy-done.3, ...), custom_call_target="tpu_custom_call" | custom-call | tf_op jit(solution)/shard_map/back/pallas_call | solution.py:578
  116.1 22.0 %dp_sum_2.1 = (bf16[128,3584]{1,0:T(8,128)(2,1)S(1)}, bf16[64,4096]{1,0:T(8,128)(2,1)S(1)}) custom-call(bf16[128,3584]{1,0:T(8,128)(2,1)S(1)} %get-tuple-element.28.refs_0_, bf16[64,4096]{1,0:T(8,128)(2,1)S(1)} %get-tuple-element.29.refs_1_), custom_call_target="tpu_custom_call" | custom-call | tf_op jit(solution)/shard_map/dp_sum_2/pallas_call | solution.py:425
  138.0 1.4 %slice_convert_fusion = (f32[64,3584]{1,0:T(8,128)}, f32[64,3584]{1,0:T(8,128)}) fusion(bf16[128,3584]{1,0:T(8,128)(2,1)S(1)} %get-tuple-element.30), kind=kLoop, calls=%fused_computation.1 | loop fusion | flops 458752 | bytes 2752512 | tf_op jit(solution)/shard_map/convert_element_type | solution.py:602
  139.4 1.0 bitcast_convert_fusion
Async XLA Ops:
  1.3 98.1 %copy-start.3 = (s32[3]{0:T(128)S(1)}, s32[3]{0:T(128)}, u32[]{:S(2)}) copy-start(s32[3]{0:T(128)} %ranks_ref.3) | copy-start | bytes 40
  81.0 18.4 %copy-start = (bf16[256,3584]{1,0:T(8,128)(2,1)S(1)}, bf16[256,3584]{1,0:T(8,128)(2,1)}, u32[]{:S(2)}) copy-start(bf16[256,3584]{1,0:T(8,128)(2,1)} %get-tuple-element.24.hid_hbm) | copy-start | bytes 5505028
  81.0 1.4 copy-start.1
  99.3 1.0 copy-start.2
